TPU v7x, 256 devices: a whole 4x4x8 slice. The times are simulated.
256 devices in a mesh: row: 4 (over y), col: 32 (over x, z), layer: 2 (over core).
Axes of the slice: x: 4, y: 4, z: 8, core: 2. Of those that a mesh axis runs over, the one named last changes fastest.
Arguments:
- xband: bfloat16 [1024, 9, 128, 128], P(('row', 'col')), may hold values from -6 to 6
- xkeep: int32 [1024, 9], P(('row', 'col')), may hold values 0 or 1
- ykeep: int32 [1024, 17], P(('row', 'col')), may hold values 0 or 1
Outputs:
- xnext: bfloat16 [1024, 9, 128, 128], P(('row', 'col'), None, 'layer')
All inputs are finite; a program needn't handle non-finite values. No bound on the sum of `xkeep` or of `ykeep` on one device may be relied on, other than what follows from the above.
Results may differ from a plain program's by a relative error of at most 0.0065.
Values may be sent and summed in bfloat16 or wider, within the bound.
A program may use at most 192 MiB of HBM per device.

v0:
```python
import functools

import jax
import jax.numpy as jnp
from jax import lax
from jax.experimental import pallas as pl
from jax.experimental.pallas import tpu as pltpu
from jax.sharding import PartitionSpec as P

B = 128
W = 4
LAST = 7
NC = 3
NZ = W - NC
PAIRS = [(a, b) for a in range(W) for b in range(a + 1)]
NP = NC * (NC + 1) // 2
WIDTH = 2 * W + 1
SUPER = W * B
HALF = B // 2
MESH = pl.DeviceIdType.MESH
BF = jnp.bfloat16
F32 = jnp.float32


def kernel(
    groups, cols, scale,
    x_hbm, xk_hbm, yk_hbm, out_ref,
    dm, do, rnm, rnn, ymo, ymm, ymp, yom, yoo, yon, ynm, yno, ymn,
    acc_mm, acc_mn, acc_o, acc_mo, acc_ynm, acc_ymn, acc_z, zs, zr, yz, cs, cm, co, fw, stg, pb, po, xk, yk, xkn, ykn, xkv, ykv,
    in_sem, k_sem, tri_s, tri_r, mid_s, mid_r, key_s, key_r, y_s, y_r, z_s, z_r, c_s, c_r,
    o_s, o_r, p_s, p_r,
):
    row, col, l = lax.axis_index("row"), lax.axis_index("col"), lax.axis_index("layer")
    group = row * cols + col
    step = 2 * l - 1

    def device(g, layer):
        g = lax.rem(g + groups, groups)
        return (g // cols, lax.rem(g, cols), layer)

    sib = (row, col, 1 - l)
    facing = device(group + step, 1 - l)
    same = device(group + step, l)
    other = device(group - step, l)
    has_n = jnp.logical_and(group + step >= 0, group + step < groups)
    has_other = jnp.logical_and(group - step >= 0, group - step < groups)

    early = jnp.logical_and(has_n, jnp.logical_and(l == 0, lax.rem(col, LAST + 1) == 0))
    beside_late = jnp.logical_and(l == 0, lax.rem(col, LAST + 1) == LAST)
    late = jnp.logical_and(has_n, jnp.logical_and(l == 1, lax.rem(col, LAST + 1) == LAST))

    barrier = pltpu.get_barrier_semaphore()
    pl.semaphore_signal(barrier, inc=1, device_id=sib, device_id_type=MESH)

    @pl.when(has_n)
    def _():
        pl.semaphore_signal(barrier, inc=1, device_id=facing, device_id_type=MESH)

    @pl.when(jnp.logical_and(has_other, jnp.logical_not(beside_late)))
    def _():
        pl.semaphore_signal(barrier, inc=1, device_id=other, device_id_type=MESH)

    b_mo, b_mn, b_om, b_op = 8 * (1 - l), 8 * l, 8 * l, 8 * (1 - l)

    def side(right, q):
        return jnp.where(right, q, 3 - q), jnp.where(right, 8 - q, 0)

    keeps = [pltpu.make_async_copy(xk_hbm, xk, k_sem.at[0]), pltpu.make_async_copy(yk_hbm, yk, k_sem.at[1])]
    loads = [
        pltpu.make_async_copy(x_hbm.at[4 * s + i], d.at[pl.ds(i, WIDTH), pl.ds(i * B, B)], in_sem.at[n, i])
        for n, (s, d) in enumerate(((l, dm), (1 - l, do)))
        for i in range(4)
    ]
    @pl.when(jnp.logical_not(late))
    def _():
        for copy in keeps + loads:
            copy.start()

    keys = [
        pltpu.make_async_remote_copy(src, dst, key_s.at[n], key_r.at[n], device_id=facing, device_id_type=MESH)
        for n, (src, dst) in enumerate(((xk_hbm, xkv), (yk_hbm, ykv)))
    ]
    tri, mid = [], []
    for q in range(4):
        i, e = side(l == 1, q)
        rows = pl.ds(pl.multiple_of(i * B, B), B)
        tri.append(pltpu.make_async_remote_copy(
            x_hbm.at[4 * l + i, pl.ds(e, q + 1)], rnm.at[pl.ds(jnp.where(l == 1, 0, i), q + 1), rows],
            tri_s.at[q], tri_r.at[q], device_id=facing, device_id_type=MESH))
    for i in range(4):
        mid.append(pltpu.make_async_remote_copy(
            x_hbm.at[4 * l + i, pl.ds(4 - i, 4)], rnn.at[:, pl.ds(i * B, B)],
            mid_s.at[i], mid_r.at[i], device_id=facing, device_id_type=MESH))

    @pl.when(jnp.logical_not(has_n))
    def _():
        rnm[...] = jnp.zeros_like(rnm)
        rnn[...] = jnp.zeros_like(rnn)
        zr[...] = jnp.zeros_like(zr)
        cm[...] = jnp.zeros_like(cm)
        xkv[...] = jnp.zeros_like(xkv)
        ykv[...] = jnp.zeros_like(ykv)

    @pl.when(jnp.logical_not(has_other))
    def _():
        co[...] = jnp.zeros_like(co)

    pl.semaphore_wait(barrier, jnp.where(has_n, jnp.where(early, 2, 3), 1))

    @pl.when(has_n)
    def _():
        for copy in keys + tri[::-1]:
            copy.start()

    @pl.when(late)
    def _():
        for copy in keeps + loads:
            copy.start()

    for d in (dm, do):
        for k in range(3):
            d[k, (k + 1) * B:, :] = jnp.zeros((SUPER - (k + 1) * B, B), BF)
            d[9 + k, : (k + 1) * B, :] = jnp.zeros(((k + 1) * B, B), BF)
    for s in range(1, 4):
        k = jnp.where(l == 1, s - 1, 4 - s)
        start = pl.multiple_of(jnp.where(l == 1, s * B, 0), B)
        rnm[k, pl.ds(start, (4 - s) * B), :] = jnp.zeros(((4 - s) * B, B), BF)

    def mask(ref, k, i, keep):
        rows = pl.ds(i * B if isinstance(i, int) else pl.multiple_of(i * B, B), B)
        ref[k, rows, :] = ref[k, rows, :] * jnp.full((B, B), keep.astype(F32), F32).astype(BF)

    def mask_rows(srow, d):
        for i in range(4):
            for g in range(WIDTH):
                mask(d, g + i, i, xk[4 * srow + i, g])

    for copy in keeps + loads[:4]:
        copy.wait()
    mask_rows(l, dm)
    for copy in loads[4:]:
        copy.wait()
    mask_rows(1 - l, do)

    def cat(ref, base=0, count=4, rows=slice(None)):
        return jnp.concatenate([ref[base + j, rows, :] for j in range(count)], axis=1)

    def lhs(*pieces):
        return jnp.concatenate([cat(*p) for p in pieces], axis=1)

    def rhs(*pieces):
        return jnp.concatenate([cat(*p) for p in pieces], axis=0)

    def dot(a, b):
        return jnp.dot(a, b, preferred_element_type=F32)

    def put(ref, value):
        for j in range(value.shape[1] // B):
            ref[j] = value[:, j * B:(j + 1) * B]

    def store_y(dst, value, table, first, h, base=0, col=0, row=0):
        for i in range(row, row + value.shape[0] // B):
            for j in range(value.shape[1] // B):
                keep = table[first + i, jnp.clip(h + col + j - i, 0, 4 * W)].astype(F32) * scale
                block = value[(i - row) * B:(i - row + 1) * B, j * B:(j + 1) * B]
                dst[base + j, i * B:(i + 1) * B, :] = (block * keep).astype(BF)

    def to_sib(src, dst, index):
        return pltpu.make_async_remote_copy(src, dst, y_s.at[index], y_r.at[index], device_id=sib, device_id_type=MESH)

    send_ymo, send_ymp, send_ymm = to_sib(ymo, yom, 0), to_sib(ymp, yon, 1), to_sib(ymm, yoo, 2)
    mo, mm, mn = (dm, b_mo), (dm, 4), (dm, b_mn)
    theirs = 4 * (1 - l)
    z_out, c_out = NC * l, NZ * (1 - l)
    z_in, c_in = NC * (1 - l), NZ * l
    send_z = pltpu.make_async_remote_copy(zs, zr, z_s, z_r, device_id=facing, device_id_type=MESH)

    put(acc_mm, dot(lhs(mo, mm), rhs((do, b_om), mm)))
    zs[...] = acc_mm[z_out].astype(BF)
    store_y(ymo, dot(lhs(mo, mm), rhs((do, 4), mo)), yk, 4 * l, 12 - 8 * l)
    send_ymo.start()
    store_y(ymp, dot(cat(*mo), cat(do, b_op)), yk, 4 * l, 16 - 16 * l)
    send_ymp.start()

    @pl.when(jnp.logical_and(has_n, jnp.logical_not(early)))
    def _():
        tri[1].wait_send()
        for copy in mid[:2]:
            copy.start()

    @pl.when(jnp.logical_and(has_n, jnp.logical_not(jnp.logical_or(early, late))))
    def _():
        for copy in mid[2:]:
            copy.start()

    put(acc_ymn, dot(cat(*mm), cat(*mn)))

    put(acc_mo, dot(cat(*mm), cat(ymo)))
    send_ymo.wait_recv()
    put(acc_o, dot(cat(*mo), cat(yom)))
    send_ymp.wait_recv()
    put(acc_mn, dot(cat(*mo), cat(yon)))

    @pl.when(early)
    def _():
        tri[1].wait_send()
        for copy in mid[:2]:
            copy.start()

    @pl.when(jnp.logical_or(early, late))
    def _():
        for copy in mid[2:]:
            copy.start()

    @pl.when(has_n)
    def _():
        for copy in keys:
            copy.wait()

    to_smem = [pltpu.make_async_copy(xkv, xkn, k_sem.at[0]), pltpu.make_async_copy(ykv, ykn, k_sem.at[1])]
    for copy in to_smem:
        copy.start()
    for copy in to_smem:
        copy.wait()

    @pl.when(has_n)
    def _():
        send_z.start()

    def mask_tri(q):
        i, e = side(l == 0, q)
        for t in range(q + 1):
            mask(rnm, jnp.where(l == 0, 0, i) + t, i, xkn[theirs + i, e + t])

    @pl.when(has_n)
    def _():
        for copy in tri[1:]:
            copy.wait_recv()

    for q in range(1, 4):
        mask_tri(q)
    part = pl.ds(pl.multiple_of(c_out * B, B), NC * B)
    value = cat(acc_mm, c_out, NC) + dot(cat(dm, b_mn + c_out, NC), cat(rnm, c_out, NC, part))
    store_y(ymm, value, yk, 4 * l, 8, c_out, c_out)
    c = dot(cat(rnm, 0, 4, part), cat(ymm, c_out, NC))

    def pick(value, first, a, b):
        block = value[a * B:(a + 1) * B, b * B:(b + 1) * B]
        return block if a == b else jnp.where(first, block, value[b * B:(b + 1) * B, a * B:(a + 1) * B])

    for n, (a, b) in enumerate(PAIRS[:NP]):
        block = pick(c, l == 0, a, b).astype(BF)
        for h in range(2):
            cs[h, n] = block[h * HALF:(h + 1) * HALF]
    def send_c(src, dst, send, recv, there):
        return pltpu.make_async_remote_copy(src, dst, c_s.at[send], c_r.at[recv], device_id=there, device_id_type=MESH)

    c_facing = send_c(cs.at[1 - l], cm, 0, 0, facing)
    c_same = send_c(cs.at[l], co, 1, 1, same)
    c_late = send_c(cs.at[l], fw, 2, 2, facing)
    c_forward = send_c(fw, co, 3, 1, sib)

    @pl.when(jnp.logical_and(has_n, jnp.logical_not(early)))
    def _():
        c_same.start()

    @pl.when(early)
    def _():
        c_late.start()

    @pl.when(has_n)
    def _():
        c_facing.start()

    @pl.when(has_n)
    def _():
        tri[0].wait_recv()

    mask_tri(0)
    store_y(ymm, acc_mm[z_out] + dot(cat(*mn), rnm[z_out]), yk, 4 * l, 8, z_out, z_out)
    send_ymm.start()
    store_y(yno, dot(cat(rnm), cat(*mo)), ykn, theirs, 16 - 16 * l)
    put(acc_ynm, dot(cat(rnm), cat(*mm)))
    acc_z[...] = dot(cat(rnm), dm[b_mn + z_in])

    def finish(cube, base, i, j):
        keep = xk[4 * l + i, base + j - i].astype(F32)
        rows = pl.ds(i * B if isinstance(i, int) else pl.multiple_of(i * B, B), B)
        own = dm[base + j, rows, :].astype(F32)
        return ((1.5 * own - (0.5 * scale) * cube) * keep).astype(BF)

    def stage(cube, base, i, j):
        block = finish(cube, base, i, j)
        low, high = block[:HALF], block[HALF:]
        out_ref[4 * l + i, base + j - i] = jnp.where(l == 0, low, high)
        stg[i, base + j - i] = jnp.where(l == 0, high, low)

    def outs(n, i, e, count):
        return pltpu.make_async_remote_copy(
            stg.at[i, pl.ds(e, count)], out_ref.at[4 * l + i, pl.ds(e, count)], o_s.at[n], o_r.at[n],
            device_id=sib, device_id_type=MESH)

    put(acc_o, cat(acc_o) + dot(cat(*mm), cat(ymm)))
    send_ymm.wait_recv()
    value = cat(acc_mo) + dot(lhs(mo, mn), rhs((yoo,), (yno,)))
    for a, b in PAIRS:
        stage(pick(value, l == 0, a, b), b_mo, jnp.where(l == 0, a, b), jnp.where(l == 0, b, a))
    out_a = []
    for q in range(4):
        i, e = side(l == 0, q)
        out_a.append(outs(q, i, e, q + 1))
    for copy in out_a:
        copy.start()

    for first in (0, 2):
        rows = slice(first * B, (first + 2) * B)

        @pl.when(has_n)
        def _(first=first):
            for copy in mid[first:first + 2]:
                copy.wait_recv()

        for i in range(first, first + 2):
            for j in range(4):
                mask(rnn, j, i, xkn[theirs + i, 4 + j - i])
        part = cat(dm, b_mn + first, 2)
        value = cat(acc_ynm, 0, 4, rows) + dot(cat(rnn, 0, 4, rows), cat(rnm))
        store_y(ynm, value, ykn, theirs, 12 - 8 * l, row=first)
        value = cat(acc_o) + dot(part, cat(ynm, 0, 4, rows))
        if first == 0:
            put(acc_o, value)
            put(acc_ymn, cat(acc_ymn) + dot(part, cat(rnn, 0, 4, rows)))
    store_y(ymn, cat(acc_ymn) + dot(part, cat(rnn, 0, 4, rows)), yk, 4 * l, 4 + 8 * l)
    c_rows = pl.ds(pl.multiple_of(c_in * B, B), NC * B)
    part_c = cat(acc_mn, c_in, NC, c_rows) + dot(cat(dm, 4, 4, c_rows), cat(ymn, c_in, NC))
    for n, (a, b) in enumerate(PAIRS[:NP]):
        i, j = jnp.where(l == 1, NZ + a, b), jnp.where(l == 1, NZ + b, a)
        block = finish(pick(part_c, l == 1, a, b), b_mn, i, j)
        for h in range(2):
            pb[h, n] = block[h * HALF:(h + 1) * HALF]
    send_p = pltpu.make_async_remote_copy(pb.at[1 - l], po, p_s, p_r, device_id=sib, device_id_type=MESH)
    send_p.start()
    out_m = []
    for i in range(4):
        for j in range(4):
            stage(value[i * B:(i + 1) * B, j * B:(j + 1) * B], 4, i, j)
        out_m.append(outs(4 + i, i, 4 - i, 4))
        out_m[i].start()
    value = acc_mn[z_in] + dot(cat(*mm), ymn[z_in])

    @pl.when(has_n)
    def _():
        send_z.wait_recv()

    store_y(yz, zr[...].astype(F32) + acc_z[...], ykn, theirs, 8, 0, z_in)
    value = value + dot(cat(*mn), yz[0])
    out_z = []
    for i in range(4):
        stage(value[i * B:(i + 1) * B], b_mn, i, z_in)
        out_z.append(outs(8 + i, i, b_mn + z_in - i, 1))
        out_z[i].start()

    send_p.wait_recv()

    def add(srow, part, term):
        for n, (a, b) in enumerate(PAIRS[:NP]):
            i = jnp.where(srow == 1, NZ + a, b)
            e = jnp.where(srow == 1, 2 * W + b - a, a - b)
            keep = xk[4 * srow + i, e].astype(F32) * (0.5 * scale)
            out_ref[4 * srow + i, e] = (part[n].astype(F32) - keep * term[n].astype(F32)).astype(BF)

    @pl.when(late)
    def _():
        c_late.wait_recv()
        c_forward.start()

    @pl.when(has_n)
    def _():
        c_facing.wait_recv()

    add(l, pb.at[l], cm)

    @pl.when(has_other)
    def _():
        c_same.wait_recv()

    add(1 - l, po, co)

    for copy in out_a + out_m + out_z:
        copy.wait()
    for copy in (send_ymo, send_ymp, send_ymm, send_p):
        copy.wait_send()

    @pl.when(has_n)
    def _():
        for copy in tri[:1] + tri[2:] + [send_z, c_facing]:
            copy.wait_send()

    @pl.when(early)
    def _():
        c_late.wait_send()

    @pl.when(jnp.logical_and(has_n, jnp.logical_not(early)))
    def _():
        c_same.wait_send()

    @pl.when(late)
    def _():
        c_forward.wait_send()

    @pl.when(has_n)
    def _():
        for copy in mid:
            copy.wait_send()


def solution(mesh):
    cols = mesh.shape["col"]
    groups = mesh.shape["row"] * cols

    def step(xband, xkeep, ykeep):
        scale = (2.0 * WIDTH * B) ** -0.5
        rows = xband.shape[0]
        dense = lambda n, dtype=BF: pltpu.VMEM((n, SUPER, B), dtype)
        sems = lambda *n: pltpu.SemaphoreType.DMA(n)
        halves = lambda *n: pltpu.VMEM((*n, HALF, B), BF)
        scratch = (
            [dense(12), dense(12)] + [dense(4)] * 11 + [dense(4, F32)] * 6
            + [pltpu.VMEM((SUPER, B), F32), pltpu.VMEM((SUPER, B), BF), pltpu.VMEM((SUPER, B), BF), dense(1)]
            + [halves(2, NP), halves(NP), halves(NP), halves(NP), halves(4, WIDTH), halves(2, NP), halves(NP)]
            + [pltpu.SMEM(a.shape, jnp.int32) for a in (xkeep, ykeep, xkeep, ykeep)]
            + [pltpu.VMEM(a.shape, jnp.int32) for a in (xkeep, ykeep)]
            + [sems(2, 4), sems(2), sems(4), sems(4), sems(4), sems(4), sems(2), sems(2), sems(3), sems(3)]
            + [sems(), sems(), sems(4), sems(3), sems(12), sems(12), sems(), sems()]
        )
        args = [pltpu.with_memory_space_constraint(a, pltpu.HBM) for a in (xband, xkeep, ykeep)]
        return pl.pallas_call(
            functools.partial(kernel, groups, cols, scale),
            out_shape=jax.ShapeDtypeStruct((rows, WIDTH, HALF, B), BF),
            in_specs=[pl.BlockSpec(memory_space=pl.ANY)] * 3,
            out_specs=pl.BlockSpec(memory_space=pltpu.VMEM),
            scratch_shapes=scratch,
            compiler_params=pltpu.CompilerParams(
                collective_id=0, has_side_effects=True, vmem_limit_bytes=40 * 2**20),
        )(*args)

    in_specs = (P(("row", "col"), None, None, None), P(("row", "col"), None), P(("row", "col"), None))
    return jax.shard_map(step, mesh=mesh, in_specs=in_specs, out_specs=P(("row", "col"), None, "layer", None), check_vma=False)
```

profile of v0, /device:TPU:25, one launch (start us, length us, event | category | flops | bytes accessed | tf_op | source)
XLA Modules:
  0.0 24.8 jit_solution(136526003532839239)
XLA Ops:
  0.0 23.8 %shard_map.37 = bf16[8,9,64,128]{3,2,1,0:T(8,128)(2,1)S(1)} custom-call(bf16[8,9,128,128]{3,2,1,0:T(8,128)(2,1)} %x_hbm.1, s32[8,9]{1,0:T(8,128)} %xk_hbm.1, s32[8,17]{1,0:T(8,128)} %yk_hbm.1), custom_call_target="tpu_custom_call" | custom-call | tf_op jit(solution)/shard_map/pallas_call | solution.py:437
  23.8 1.0 %copy.5 = bf16[8,9,64,128]{3,2,1,0:T(8,128)(2,1)} copy(bf16[8,9,64,128]{3,2,1,0:T(8,128)(2,1)S(1)} %shard_map.37) | data formatting | bytes 2359296
where the time goes:
time: 24.9 us; the launch traced here: 24.8 us
  Pallas kernels  23.8 us (96%)
  local copies, waits for them, and re-layouts  1.02 us (4%)
    pallas_call x1, Pallas kernels, step(): pl.pallas_call(functools.partial(kernel, groups, cols, scale), out_shape=...  23.8 us
    unnamed x1, local copies, waits for them, and re-layouts  1.02 us

commit v1 on v0

--- a/solution.py
+++ b/solution.py
@@ -109,7 +109,7 @@
 
     @pl.when(has_n)
     def _():
-        for copy in keys + tri[::-1]:
+        for copy in keys + tri[::-1] + mid:
             copy.start()
 
     @pl.when(late)
@@ -182,17 +182,6 @@
     store_y(ymp, dot(cat(*mo), cat(do, b_op)), yk, 4 * l, 16 - 16 * l)
     send_ymp.start()
 
-    @pl.when(jnp.logical_and(has_n, jnp.logical_not(early)))
-    def _():
-        tri[1].wait_send()
-        for copy in mid[:2]:
-            copy.start()
-
-    @pl.when(jnp.logical_and(has_n, jnp.logical_not(jnp.logical_or(early, late))))
-    def _():
-        for copy in mid[2:]:
-            copy.start()
-
     put(acc_ymn, dot(cat(*mm), cat(*mn)))
 
     put(acc_mo, dot(cat(*mm), cat(ymo)))
@@ -200,17 +189,6 @@
     put(acc_o, dot(cat(*mo), cat(yom)))
     send_ymp.wait_recv()
     put(acc_mn, dot(cat(*mo), cat(yon)))
-
-    @pl.when(early)
-    def _():
-        tri[1].wait_send()
-        for copy in mid[:2]:
-            copy.start()
-
-    @pl.when(jnp.logical_or(early, late))
-    def _():
-        for copy in mid[2:]:
-            copy.start()
 
     @pl.when(has_n)
     def _():
@@ -393,7 +371,7 @@
 
     @pl.when(has_n)
     def _():
-        for copy in tri[:1] + tri[2:] + [send_z, c_facing]:
+        for copy in tri + [send_z, c_facing]:
             copy.wait_send()
 
     @pl.when(early)

time: 24.9 us -> 24.4 us (0.980)
  Pallas kernels: 23.8 us -> 23.3 us
    pallas_call x1, Pallas kernels: 23.8 us -> 23.3 us  [step(): pl.pallas_call(functools.partial(kernel, groups, cols, scale), out_shape=...]
where the time goes in v1:
time: 24.4 us; the launch traced here: 24.3 us
  Pallas kernels  23.3 us (95%)
  local copies, waits for them, and re-layouts  1.02 us (4%)
    pallas_call x1, Pallas kernels, step(): pl.pallas_call(functools.partial(kernel, groups, cols, scale), out_shape=...  23.3 us
    unnamed x1, local copies, waits for them, and re-layouts  1.02 us

profile of v1, /device:TPU:25, one launch (start us, length us, event | category | flops | bytes accessed | tf_op | source)
XLA Modules:
  0.0 24.3 jit_solution(14491962759958769393)
XLA Ops:
  0.0 23.3 %shard_map.37 = bf16[8,9,64,128]{3,2,1,0:T(8,128)(2,1)S(1)} custom-call(bf16[8,9,128,128]{3,2,1,0:T(8,128)(2,1)} %x_hbm.1, s32[8,9]{1,0:T(8,128)} %xk_hbm.1, s32[8,17]{1,0:T(8,128)} %yk_hbm.1), custom_call_target="tpu_custom_call" | custom-call | tf_op jit(solution)/shard_map/pallas_call | solution.py:415
  23.3 1.0 %copy.5 = bf16[8,9,64,128]{3,2,1,0:T(8,128)(2,1)} copy(bf16[8,9,64,128]{3,2,1,0:T(8,128)(2,1)S(1)} %shard_map.37) | data formatting | bytes 2359296
